TPU v7x, 32 devices: a whole 2x2x4 slice. The times are simulated.
32 devices in a mesh: groups: 2 (over x), blk: 16 (over z, y, core).
Axes of the slice: x: 2, y: 2, z: 4, core: 2. Of those that a mesh axis runs over, the one named last changes fastest.
Arguments:
- tokens: bfloat16 [256, 6144], P(('groups', 'blk')), parts along dimension 0, may hold values from -6 to 6
- norm_gain: float32 [6144], replicated, may hold values from 0.1 to 1.9
- w_expand: bfloat16 [6144, 24576], P(None, 'blk'), may hold values from -0.078125 to 0.078125
- b_expand: float32 [24576], P('blk'), may hold values from -3 to 3
- w_project: bfloat16 [24576, 6144], P('blk'), may hold values from -0.0390625 to 0.0390625
- b_project: float32 [6144], replicated, may hold values from -3 to 3
Outputs:
- mixed: bfloat16 [256, 6144], P(('groups', 'blk')), parts along dimension 0
There are 2 independent parts, one for each index of `groups`. A program takes and returns all parts, laid end to end along the dimension named above; an argument that names none is the same for every part. Nothing has to cross between parts.
All inputs are finite; a program needn't handle non-finite values.
Results may differ from a plain program's by a relative error of at most 0.0055.
Values may be sent and summed in bfloat16 or wider, within the bound.
A program may use at most 128 MiB of HBM per device.

v0:
```python
import jax
import jax.numpy as jnp
from jax import lax
from jax.sharding import PartitionSpec as P


def gelu_tanh(value):
    return 0.5 * value * (1.0 + jnp.tanh(0.7978845608 * (value + 0.044715 * value * value * value)))


def on_device(tokens, norm_gain, w_expand, b_expand, w_project, b_project):
    wide = tokens.astype(jnp.float32)
    row_mean = jnp.mean(wide, axis=1, keepdims=True)
    centred = wide - row_mean
    row_spread = jnp.mean(centred * centred, axis=1, keepdims=True)
    normed = (centred / jnp.sqrt(row_spread + 1e-06) * norm_gain).astype(jnp.bfloat16)
    inner = (
        jnp.dot(
            lax.all_gather(normed, "blk", axis=0, tiled=True),
            w_expand,
            preferred_element_type=jnp.float32,
        )
        + b_expand
    )
    hidden = gelu_tanh(inner).astype(jnp.bfloat16)
    summed = lax.psum_scatter(
        jnp.dot(hidden, w_project, preferred_element_type=jnp.float32),
        "blk",
        scatter_dimension=0,
        tiled=True,
    )
    mixed = (summed + b_project).astype(jnp.bfloat16)
    return mixed


def solution(mesh):
    placed = (P(("groups", "blk"), None), P(), P(None, "blk"), P("blk"), P("blk", None), P())
    return jax.shard_map(
        on_device, mesh=mesh, in_specs=placed, out_specs=P(("groups", "blk"), None), check_vma=False
    )
```

profile of v0, /device:TPU:0, one launch (start us, length us, event | category | flops | bytes accessed | tf_op | source)
XLA Modules:
  0.0 143.1 jit_solution(8380594404417822526)
XLA Ops:
  6.5 0.0 all-gather.2.cloned.1.call-start
  6.5 1.1 convert_reduce_fusion
  7.6 1.1 fusion.7
  8.7 1.6 %fusion.9 = bf16[8,6144]{1,0:T(8,128)(2,1)} fusion(bf16[8,6144]{1,0:T(8,128)(2,1)} %param.6, f32[6144]{0:T(1024)} %param.7, f32[8]{0:T(128)S(1)} %add_sqrt_fusion, f32[8]{0:T(128)S(1)} %broadcast_multiply_fusion), kind=kLoop, calls=%fused_computation.13 | loop fusion | flops 245760 | bytes 221248 | tf_op jit(solution)/shard_map/convert_element_type | solution.py:16
  10.4 0.0 all-gather.2.cloned.1.call-update
  10.4 0.0 reduce-scatter.2.cloned.1.call-start
  10.4 42.5 %all-gather.2.cloned.1.call-done = bf16[128,6144]{1,0:T(8,128)(2,1)} async-done(((bf16[8,6144]{1,0:T(8,128)(2,1)}), bf16[128,6144]{1,0:T(8,128)(2,1)}) %all-gather.2.cloned.1.call-update) | async-done | bytes 1572880 | tf_op jit(solution)/shard_map/all_gather | solution.py:19
  52.9 0.0 copy-start
  52.9 9.8 %fusion.4 = bf16[128,1536]{1,0:T(8,128)(2,1)S(1)} fusion(bf16[128,6144]{1,0:T(8,128)(2,1)} %all-gather.2.cloned.1.call-done, bf16[6144,1536]{1,0:T(8,128)(2,1)} %param.8, f32[1536]{0:T(1024)} %param.9), kind=kOutput, calls=%fused_computation.6 | convolution fusion | flops 2417885184 | bytes 20846592 | tf_op jit(solution)/shard_map/dot_general | solution.py:18
  62.7 2.4 %copy-done = bf16[1536,6144]{1,0:T(8,128)(2,1)S(1)} copy-done((bf16[1536,6144]{1,0:T(8,128)(2,1)S(1)}, bf16[1536,6144]{1,0:T(8,128)(2,1)}, u32[]{:S(2)}) %copy-start) | copy-done | bytes 18874392
  65.1 0.0 copy-start.1
  65.1 4.3 %fusion.10 = f32[128,6144]{1,0:T(8,128)} fusion(bf16[128,1536]{1,0:T(8,128)(2,1)S(1)} %fusion.4, bf16[1536,6144]{1,0:T(8,128)(2,1)S(1)} %copy-done), kind=kOutput, calls=%fused_computation.17 | convolution fusion | flops 2415919104 | bytes 22413312 | tf_op jit(solution)/shard_map/dot_general | solution.py:27
  69.4 0.0 reduce-scatter.2.cloned.1.call-update
  69.4 65.3 %reduce-scatter.2.cloned.1.call-done = f32[8,6144]{1,0:T(8,128)} async-done(((f32[128,6144]{1,0:T(8,128)}), f32[8,6144]{1,0:T(8,128)}) %reduce-scatter.2.cloned.1.call-update) | async-done | bytes 196624 | tf_op jit(solution)/shard_map/reduce_scatter | solution.py:26
  134.7 0.0 copy-done.1
  134.7 1.6 %add_convert_fusion = bf16[8,6144]{1,0:T(8,128)(2,1)} fusion(f32[8,6144]{1,0:T(8,128)} %reduce-scatter.2.cloned.1.call-done, f32[6144]{0:T(1024)S(1)} %copy-done.1), kind=kLoop, calls=%fused_computation.14 | loop fusion | flops 98304 | bytes 319488 | tf_op jit(solution)/shard_map/convert_element_type | solution.py:32
  (2 shorter events, 0.0 us)
Async XLA Ops:
  6.5 46.4 %all-gather.2.cloned.1.call-start = ((), (), s32[]{:S(2)}) async-start(), calls=%async_computation.1 | async-start | bytes 1671168 | tf_op jit(solution)/shard_map/all_gather | solution.py:19
  10.4 124.3 %reduce-scatter.2.cloned.1.call-start = ((), (), s32[]{:S(2)}) async-start(), calls=%async_computation.2 | async-start | bytes 3342336 | tf_op jit(solution)/shard_map/reduce_scatter | solution.py:26
  52.9 12.2 %copy-start = (bf16[1536,6144]{1,0:T(8,128)(2,1)S(1)}, bf16[1536,6144]{1,0:T(8,128)(2,1)}, u32[]{:S(2)}) copy-start(bf16[1536,6144]{1,0:T(8,128)(2,1)} %param.10) | copy-start | bytes 56623108
  65.1 69.6 %copy-start.1 = (f32[6144]{0:T(1024)S(1)}, f32[6144]{0:T(1024)}, u32[]{:S(2)}) copy-start(f32[6144]{0:T(1024)} %param.11) | copy-start | bytes 73732
Sparse Core Ops, SparseCore 0:
  10.5 42.3 all-gather.1
  69.6 65.0 reduce-scatter.1
where the time goes:
time: 143 us
  waiting for transfers between devices  108 us (76%)
  matrix products  14 us (10%)
  between operations  13.4 us (9%)
  other arithmetic  5.42 us (4%)
  local copies, waits for them, and re-layouts  2.44 us (2%)
    reduce_scatter x1, waiting for transfers between devices, on_device(): lax.psum_scatter(jnp.dot(hidden, w_project, preferred_element_type=jnp.fl...  65.3 us
    all_gather x1, waiting for transfers between devices, on_device(): lax.all_gather(normed, 'blk', axis=0, tiled=True)  42.5 us
    dot_general x1, matrix products, on_device(): jnp.dot(lax.all_gather(normed, 'blk', axis=0, tiled=True), w_expand, pref...  9.76 us
    dot_general x1, matrix products, on_device(): jnp.dot(hidden, w_project, preferred_element_type=jnp.float32)  4.28 us
  transfers between devices with their start and end apart: 2, of which 2 were waited for; matrix products, arithmetic and copies ran while one was open for 0% of the time, Pallas kernels for 0%

commit v1 on v0

v1 whole, which is shorter than its diff:
```python
import functools

import jax
import jax.numpy as jnp
from jax import lax
from jax.experimental import pallas as pl
from jax.experimental.pallas import tpu as pltpu
from jax.sharding import PartitionSpec as P

F32, BF16 = jnp.float32, jnp.bfloat16
CHUNKS = 2


def gelu_tanh(value):
    return 0.5 * value * (1.0 + jnp.tanh(0.7978845608 * (value + 0.044715 * value * value * value)))


def tile_of(size, most=512):
    return max(t for t in range(128, most + 1, 128) if size % t == 0)


def chip_at(place, chips):
    if chips > 8:
        return place
    half = chips // 2
    down = lax.div(place, half)
    return (1 - down) * 2 * place + down * (2 * (chips - 1 - place) + 1)


def place_of(chip, chips):
    if chips > 8:
        return chip
    high, low = lax.div(chip, 2), lax.rem(chip, 2)
    return (1 - low) * high + low * (chips - 1 - high)


def kernel(
    n, wire, tok, gain, b1, b2, w1, w2, out,
    w1v, w2v, swap, xbuf, hid, snd, sib_in, own, ring_in, ring_out, fin, fin_in,
    w1_sem, w2_sem, swap_sem, ag_send, ag_recv, fw_send, fw_recv, sib_send, sib_recv, rs_send, rs_recv, fin_send, fin_recv,
):
    rows, width = tok.shape
    pair = 2 * rows
    chips = n // 2
    parts = 2 * CHUNKS
    wide = width // parts
    tokens = rows * n
    units = w1.shape[1]

    me = lax.axis_index("blk")
    core, chip = lax.rem(me, 2), lax.div(me, 2)
    place = place_of(chip, chips)
    step_by = 1 - 2 * core

    def around(k):
        return chip_at(lax.rem(place + step_by * k + 2 * chips, chips), chips)

    following, previous = around(1) * 2 + core, around(-1) * 2 + core
    sibling = chip * 2 + 1 - core

    def send(src, dst, send_sem, recv_sem, to):
        return pltpu.make_async_remote_copy(
            src_ref=src, dst_ref=dst, send_sem=send_sem, recv_sem=recv_sem,
            device_id={"blk": to}, device_id_type=pl.DeviceIdType.MESH,
        )

    barrier = pltpu.get_barrier_semaphore()
    for other in (following, previous, sibling):
        pl.semaphore_signal(barrier, inc=1, device_id={"blk": other}, device_id_type=pl.DeviceIdType.MESH)

    def w1_copy(g):
        at = pl.ds(g * wide, wide)
        return pltpu.make_async_copy(w1.at[at], w1v.at[at], w1_sem.at[g])

    def w2_copy(k):
        j, mine = k % CHUNKS, k // CHUNKS
        g = (core if mine else 1 - core) * CHUNKS + j
        at = pl.ds(pl.multiple_of(g * wide, wide), wide)
        return pltpu.make_async_copy(w2.at[:, at], w2v.at[:, at], w2_sem.at[k])

    for g in range(parts):
        w1_copy(g).start()
    for k in range(parts):
        w2_copy(k).start()

    x = tok[...].astype(F32)
    mean = jnp.mean(x, axis=1, keepdims=True)
    centred = x - mean
    spread = jnp.mean(centred * centred, axis=1, keepdims=True)
    normed = (centred / jnp.sqrt(spread + 1e-06) * gain[...]).astype(BF16).astype(F32)
    swap[core] = normed

    pl.semaphore_wait(barrier, 3)
    swapped = send(swap.at[core], swap.at[core], swap_sem.at[0], swap_sem.at[1], sibling)
    swapped.start()
    send(swap.at[1 - core], swap.at[1 - core], swap_sem.at[0], swap_sem.at[1], sibling).wait_recv()

    def rows_of(where):
        return pl.ds(pl.multiple_of(where * pair, pair), pair)

    both = jnp.concatenate([swap[0], swap[1]], axis=0).astype(BF16)
    for g in range(parts):
        xbuf[g, rows_of(chip), :] = both[:, g * wide:(g + 1) * wide]

    def ag(s, j, where, to, send_sem, recv_sem, half):
        block = xbuf.at[half * CHUNKS + j, rows_of(where)]
        return send(block, block, send_sem.at[s, j], recv_sem.at[s, j], to)

    for j in range(CHUNKS):
        ag(0, j, chip, following, ag_send, ag_recv, core).start()

    @pl.loop(1, chips)
    def _(s):
        where = around(-s)
        for j in range(CHUNKS):
            ag(s - 1, j, where, following, ag_send, ag_recv, core).wait_recv()

            @pl.when(s < chips - 1)
            def _():
                ag(s, j, where, following, ag_send, ag_recv, core).start()

            ag(s - 1, j, where, sibling, fw_send, fw_recv, core).start()

    for g in range(parts):
        w1_copy(g).wait()

    @pl.loop(1, chips)
    def _(s):
        for j in range(CHUNKS):
            ag(s - 1, j, around(s), sibling, fw_send, fw_recv, 1 - core).wait_recv()

    tile = tile_of(units)

    @pl.loop(0, units // tile)
    def _(t):
        at = pl.ds(pl.multiple_of(t * tile, tile), tile)
        total = jnp.dot(xbuf[0], w1v[0:wide, at], preferred_element_type=F32)
        for g in range(1, parts):
            total += jnp.dot(xbuf[g], w1v[g * wide:(g + 1) * wide, at], preferred_element_type=F32)
        hid[:, at] = gelu_tanh(total + b1[:, at]).astype(BF16)

    cut = tile_of(wide)

    def project(half, j, store):
        @pl.loop(0, wide // cut)
        def _(t):
            at = pl.ds(pl.multiple_of(t * cut, cut), cut)
            start = (half * CHUNKS + j) * wide + t * cut
            cols = pl.ds(pl.multiple_of(start, cut), cut)
            store(at, jnp.dot(hid[...], w2v[:, cols], preferred_element_type=F32))

    def sib_copy(j):
        return send(snd.at[j], sib_in.at[j], sib_send.at[j], sib_recv.at[j], sibling)

    for j in range(CHUNKS):
        w2_copy(j).wait()

        def keep_theirs(at, value, j=j):
            snd[j, :, at] = value.astype(wire)

        project(1 - core, j, keep_theirs)
        sib_copy(j).start()

    def rs_copy(s, j):
        return send(ring_out.at[s, j], ring_in.at[s, j], rs_send.at[s, j], rs_recv.at[s, j], following)

    def ours(j, where):
        return own[j, rows_of(where), :] + sib_in[j, rows_of(where), :].astype(F32)

    for j in range(CHUNKS):
        w2_copy(CHUNKS + j).wait()

        def keep_own(at, value, j=j):
            own[j, :, at] = value

        project(core, j, keep_own)
        sib_copy(j).wait_recv()
        ring_out[0, j] = ours(j, around(-1)).astype(wire)
        rs_copy(0, j).start()

    @pl.loop(1, chips - 1)
    def _(s):
        where = around(-s - 1)
        for j in range(CHUNKS):
            rs_copy(s - 1, j).wait_recv()
            ring_out[s, j] = (ours(j, where) + ring_in[s - 1, j].astype(F32)).astype(wire)
            rs_copy(s, j).start()

    def fin_copy(j):
        return send(fin.at[j, 1 - core], fin_in.at[j], fin_send.at[j], fin_recv.at[j], sibling)

    for j in range(CHUNKS):
        rs_copy(chips - 2, j).wait_recv()
        total = ours(j, chip) + ring_in[chips - 2, j].astype(F32)
        fin[j, 0] = total[:rows]
        fin[j, 1] = total[rows:]
        fin_copy(j).start()
    for j in range(CHUNKS):
        fin_copy(j).wait_recv()
    for g in range(parts):
        at = slice(g * wide, (g + 1) * wide)
        j = g % CHUNKS
        total = jnp.where(core == g // CHUNKS, fin[j, core], fin_in[j])
        out[:, at] = (total + b2[:, at]).astype(BF16)

    swapped.wait_send()
    for j in range(CHUNKS):
        sib_copy(j).wait_send()
        fin_copy(j).wait_send()

    @pl.loop(0, chips - 1)
    def _(s):
        for j in range(CHUNKS):
            ag(s, j, chip, following, ag_send, ag_recv, core).wait_send()
            ag(s, j, chip, sibling, fw_send, fw_recv, core).wait_send()
            rs_copy(s, j).wait_send()


def on_device(n, tokens, norm_gain, w_expand, b_expand, w_project, b_project):
    rows, width = tokens.shape
    units = w_expand.shape[1]
    chips = n // 2
    pair, total = 2 * rows, rows * n
    wide = width // (2 * CHUNKS)
    wire = BF16 if chips <= 8 else F32
    dma = pltpu.SemaphoreType.DMA
    vmem = pl.BlockSpec(memory_space=pltpu.VMEM)
    hbm = pl.BlockSpec(memory_space=pl.ANY)
    return pl.pallas_call(
        functools.partial(kernel, n, wire),
        out_shape=jax.ShapeDtypeStruct((rows, width), BF16),
        in_specs=[vmem] * 4 + [hbm] * 2,
        out_specs=vmem,
        scratch_shapes=[
            pltpu.VMEM((width, units), BF16),
            pltpu.VMEM((units, width), BF16),
            pltpu.VMEM((2, rows, width), F32),
            pltpu.VMEM((2 * CHUNKS, total, wide), BF16),
            pltpu.VMEM((total, units), BF16),
            pltpu.VMEM((CHUNKS, total, wide), wire),
            pltpu.VMEM((CHUNKS, total, wide), wire),
            pltpu.VMEM((CHUNKS, total, wide), F32),
            pltpu.VMEM((chips - 1, CHUNKS, pair, wide), wire),
            pltpu.VMEM((chips - 1, CHUNKS, pair, wide), wire),
            pltpu.VMEM((CHUNKS, 2, rows, wide), F32),
            pltpu.VMEM((CHUNKS, rows, wide), F32),
            dma((2 * CHUNKS,)),
            dma((2 * CHUNKS,)),
            dma((2,)),
            dma((chips - 1, CHUNKS)),
            dma((chips - 1, CHUNKS)),
            dma((chips - 1, CHUNKS)),
            dma((chips - 1, CHUNKS)),
            dma((CHUNKS,)),
            dma((CHUNKS,)),
            dma((chips - 1, CHUNKS)),
            dma((chips - 1, CHUNKS)),
            dma((CHUNKS,)),
            dma((CHUNKS,)),
        ],
        compiler_params=pltpu.CompilerParams(
            collective_id=0, has_side_effects=True, vmem_limit_bytes=60 * 1024 * 1024
        ),
    )(tokens, norm_gain[None], b_expand[None], b_project[None], w_expand, w_project)


def solution(mesh):
    placed = (P(("groups", "blk"), None), P(), P(None, "blk"), P("blk"), P("blk", None), P())
    return jax.shard_map(
        functools.partial(on_device, mesh.shape["blk"]),
        mesh=mesh, in_specs=placed, out_specs=P(("groups", "blk"), None), check_vma=False,
    )
```

time: 143 us -> 62.8 us (0.44)
  waiting for transfers between devices: 108 us -> 0 us
  Pallas kernels: 0 us -> 59.8 us
  matrix products: 14 us -> 0 us
  between operations: 13.4 us -> 0.01 us
  other arithmetic: 5.42 us -> 0 us
    reduce_scatter x1 -> x0, waiting for transfers between devices: 65.3 us -> none  [on_device(): lax.psum_scatter(jnp.dot(hidden, w_project, preferred_element_type=jnp.fl...]
    pallas_call x0 -> x1, Pallas kernels: none -> 59.8 us  [on_device(): pl.pallas_call(functools.partial(kernel, n, wire), out_shape=jax.ShapeDty...]
    all_gather x1 -> x0, waiting for transfers between devices: 42.5 us -> none  [on_device(): lax.all_gather(normed, 'blk', axis=0, tiled=True)]
    dot_general x2 -> x0, matrix products: 14 us -> none  [the longest x1 9.76 us: on_device(): jnp.dot(lax.all_gather(normed, 'blk', axis=0, tiled=True), w_expand, pref...]
    convert_element_type x2 -> x0, other arithmetic: 3.22 us -> none  [the longest x1 1.64 us: on_device(): (centred / jnp.sqrt(row_spread + 1e-06) * norm_gain).astype(jnp.bfloat16)]
    reduce_sum x2 -> x0, other arithmetic: 2.18 us -> none  [the longest x1 1.13 us: on_device(): row_spread = jnp.mean(centred * centred, axis=1, keepdims=True)]
  transfers between devices with their start and end apart: 2 -> 0, of which waited for: 2 -> 0; matrix products, arithmetic and copies ran while one was open for 0% -> 0% of each run, Pallas kernels for 0% -> 0%
where the time goes in v1:
time: 62.8 us; the launch traced here: 62.6 us
  Pallas kernels  59.8 us (95%)
  local copies, waits for them, and re-layouts  2.83 us (5%)
    pallas_call x1, Pallas kernels, on_device(): pl.pallas_call(functools.partial(kernel, n, wire), out_shape=jax.ShapeDty...  59.8 us
    unnamed x1, local copies, waits for them, and re-layouts  1.54 us
    broadcast_in_dim x1, local copies, waits for them, and re-layouts, on_device(): b_expand[None]  1.29 us

profile of v1, /device:TPU:0, one launch (start us, length us, event | category | flops | bytes accessed | tf_op | source)
XLA Modules:
  0.0 62.6 jit_solution(15334627715314580090)
XLA Ops:
  0.0 1.3 %broadcast_in_dim.10.b1 = f32[1,1536]{1,0:T(1,128)} reshape(f32[1536]{0:T(1024)} %param.9) | data formatting | bytes 12288 | tf_op jit(solution)/shard_map/broadcast_in_dim | solution.py:264
  1.3 59.8 %shard_map.64 = bf16[8,6144]{1,0:T(8,128)(2,1)} custom-call(bf16[8,6144]{1,0:T(8,128)(2,1)} %tok.1, f32[1,6144]{1,0:T(1,128)} %bitcast.2, f32[1,1536]{1,0:T(1,128)} %broadcast_in_dim.10.b1, f32[1,6144]{1,0:T(1,128)} %bitcast.3, bf16[6144,1536]{1,0:T(8,128)(2,1)} %w1.1, bf16[1536,6144]{1,0:T(8,128)(2,1)} %w2.1), custom_call_target="tpu_custom_call" | custom-call | tf_op jit(solution)/shard_map/pallas_call | solution.py:229
  61.1 1.5 %copy.8 = bf16[8,6144]{1,0:T(8,128)(2,1)} copy(bf16[8,6144]{1,0:T(8,128)(2,1)} %shard_map.64) | data formatting | bytes 196608

commit v2 on v1

v2 whole, which is shorter than its diff:
```python
import functools

import jax
import jax.numpy as jnp
from jax import lax
from jax.experimental import pallas as pl
from jax.experimental.pallas import tpu as pltpu
from jax.sharding import PartitionSpec as P

F32, BF16 = jnp.float32, jnp.bfloat16
CHUNKS = 2


def gelu_tanh(value):
    return 0.5 * value * (1.0 + jnp.tanh(0.7978845608 * (value + 0.044715 * value * value * value)))


def tile_of(size, most=768):
    step = 256 if size % 256 == 0 else 128
    return max(t for t in range(step, most + 1, step) if size % t == 0)


def chip_at(place, chips):
    if chips > 8:
        return place
    half = chips // 2
    down = lax.div(place, half)
    return (1 - down) * 2 * place + down * (2 * (chips - 1 - place) + 1)


def place_of(chip, chips):
    if chips > 8:
        return chip
    high, low = lax.div(chip, 2), lax.rem(chip, 2)
    return (1 - low) * high + low * (chips - 1 - high)


def kernel(
    n, tok, gain, b1, b2, w1, w2, out,
    w1v, w2v, xin, lhs, hid, snd, sib_in, own, ring_in, ring_out, fin, fin_in,
    w1_sem, w2_sem, ag_send, ag_recv, fw_send, fw_recv, sib_send, sib_recv, rs_send, rs_recv, fin_send, fin_recv,
):
    rows, width = tok.shape
    pair = 2 * rows
    chips = n // 2
    far = chips // 2
    half = width // 2
    wide = half // CHUNKS
    units = w1.shape[1]
    wire = ring_in.dtype
    ways = (0, 1)

    me = lax.axis_index("blk")
    core, chip = lax.rem(me, 2), lax.div(me, 2)
    place = place_of(chip, chips)

    def around(k):
        return chip_at(lax.rem(place + k + 2 * chips, chips), chips)

    sign = (1, -1)
    ahead = [around(sign[w]) * 2 + core for w in ways]
    sibling = chip * 2 + 1 - core

    def takes(way, j):
        return (j % 2) == way

    def send(src, dst, send_sem, recv_sem, to):
        return pltpu.make_async_remote_copy(
            src_ref=src, dst_ref=dst, send_sem=send_sem, recv_sem=recv_sem,
            device_id={"blk": to}, device_id_type=pl.DeviceIdType.MESH,
        )

    barrier = pltpu.get_barrier_semaphore()
    for other in (*ahead, sibling):
        pl.semaphore_signal(barrier, inc=1, device_id={"blk": other}, device_id_type=pl.DeviceIdType.MESH)

    def w1_copy(h):
        at = pl.ds(h * half, half)
        return pltpu.make_async_copy(w1.at[at], w1v.at[at], w1_sem.at[h])

    def w2_copy(h):
        at = pl.ds(pl.multiple_of((core if h else 1 - core) * half, half), half)
        return pltpu.make_async_copy(w2.at[:, at], w2v.at[:, at], w2_sem.at[h])

    for h in ways:
        w1_copy(h).start()
    for h in ways:
        w2_copy(h).start()

    x = tok[...].astype(F32)
    mean = jnp.mean(x, axis=1, keepdims=True)
    centred = x - mean
    spread = jnp.mean(centred * centred, axis=1, keepdims=True)
    normed = centred / jnp.sqrt(spread + 1e-06) * gain[...]
    folded = jnp.concatenate([normed[:, :half], normed[:, half:]], axis=0).astype(BF16)
    for j in range(CHUNKS):
        xin[me, j] = folded[:, j * wide:(j + 1) * wide]

    pl.semaphore_wait(barrier, 3)

    def ag(way, s, j, where):
        block = xin.at[where * 2 + core, j]
        return send(block, block, ag_send.at[way, s, j], ag_recv.at[way, s, j], ahead[way])

    def fw(way, s, j, where, side):
        block = xin.at[where * 2 + side, j]
        return send(block, block, fw_send.at[way, s, j], fw_recv.at[way, s, j], sibling)

    def rows_of(where):
        return pl.ds(pl.multiple_of(where * pair, pair), pair)

    def assemble(where, chunks):
        for j in chunks:
            first, second = xin[where * 2, j].astype(F32), xin[where * 2 + 1, j].astype(F32)
            at = slice(j * wide, (j + 1) * wide)
            lhs[0, rows_of(where), at] = jnp.concatenate([first[:rows], second[:rows]], axis=0).astype(BF16)
            lhs[1, rows_of(where), at] = jnp.concatenate([first[rows:], second[rows:]], axis=0).astype(BF16)

    every = range(CHUNKS)
    for j in every:
        for way in ways:
            ag(way, 0, j, chip).start()
    for j in every:
        fw(0, 0, j, chip, core).start()

    def gather(s, last, next_last):
        for j in every:
            for way in ways:
                if last and not takes(way, j):
                    continue
                where = around(-sign[way] * s)
                ag(way, s - 1, j, where).wait_recv()
                if not last and (not next_last or takes(way, j)):
                    ag(way, s, j, where).start()
                fw(way, s, j, where, core).start()

    def take(s, last):
        for way in ways:
            where = around(-sign[way] * s)
            chunks = [j for j in every if not last or takes(way, j)]
            for j in chunks:
                fw(way, s, j, where, 1 - core).wait_recv()
            assemble(where, chunks)

    gather(1, False, far == 2)
    for j in every:
        fw(0, 0, j, chip, 1 - core).wait_recv()
    assemble(chip, every)

    @pl.loop(2, far - 1)
    def _(s):
        gather(s, False, False)
        take(s - 1, False)

    if far > 2:
        gather(far - 1, False, True)
        take(far - 2, False)
    gather(far, True, False)
    take(far - 1, False)
    take(far, True)

    for h in ways:
        w1_copy(h).wait()

    tile = tile_of(units)

    @pl.loop(0, units // tile)
    def _(t):
        at = pl.ds(pl.multiple_of(t * tile, tile), tile)
        total = jnp.dot(lhs[0], w1v[:half, at], preferred_element_type=F32)
        total += jnp.dot(lhs[1], w1v[half:, at], preferred_element_type=F32)
        hid[:, at] = gelu_tanh(total + b1[:, at]).astype(BF16)

    cut = tile_of(wide)

    def project(side, j, store):
        @pl.loop(0, wide // cut)
        def _(t):
            at = pl.ds(pl.multiple_of(t * cut, cut), cut)
            cols = pl.ds(pl.multiple_of(side * half + j * wide + t * cut, cut), cut)
            store(at, jnp.dot(hid[...], w2v[:, cols], preferred_element_type=F32))

    def sib_copy(j):
        return send(snd.at[j], sib_in.at[j], sib_send.at[j], sib_recv.at[j], sibling)

    w2_copy(0).wait()
    for j in every:

        def keep_theirs(at, value, j=j):
            snd[j, :, at] = value.astype(BF16)

        project(1 - core, j, keep_theirs)
        sib_copy(j).start()

    def rs(way, k, j):
        return send(
            ring_out.at[way, k - 1, j], ring_in.at[way, k - 1, j],
            rs_send.at[way, k - 1, j], rs_recv.at[way, k - 1, j], ahead[way],
        )

    def ours(j, where):
        return own[j, rows_of(where), :] + sib_in[j, rows_of(where), :].astype(F32)

    def pass_on(way, k, j, more):
        total = ours(j, around(sign[way] * k))
        if more:
            rs(way, k + 1, j).wait_recv()
            total += ring_in[way, k, j].astype(F32)
        ring_out[way, k - 1, j] = total.astype(wire)
        rs(way, k, j).start()

    w2_copy(1).wait()
    for j in every:

        def keep_own(at, value, j=j):
            own[j, :, at] = value

        project(core, j, keep_own)
        sib_copy(j).wait_recv()
        for way in ways:
            if takes(way, j):
                pass_on(way, far, j, False)
        for way in ways:
            if not takes(way, j):
                pass_on(way, far - 1, j, False)

    for j in every:
        for way in ways:
            if takes(way, j):
                pass_on(way, far - 1, j, True)

    @pl.loop(2, far)
    def _(s):
        for j in every:
            for way in ways:
                pass_on(way, far - s, j, True)

    def fin_copy(j):
        return send(fin.at[j, 1 - core], fin_in.at[j], fin_send.at[j], fin_recv.at[j], sibling)

    for j in every:
        total = ours(j, chip)
        for way in ways:
            rs(way, 1, j).wait_recv()
            total += ring_in[way, 0, j].astype(F32)
        fin[j, 0] = total[:rows]
        fin[j, 1] = total[rows:]
        fin_copy(j).start()
    for j in every:
        fin_copy(j).wait_recv()
    for g in range(2 * CHUNKS):
        at = slice(g * wide, (g + 1) * wide)
        j = g % CHUNKS
        total = jnp.where(core == g // CHUNKS, fin[j, core], fin_in[j])
        out[:, at] = (total + b2[:, at]).astype(BF16)

    def sent(s, last):
        for j in every:
            for way in ways:
                if not last or takes(way, j):
                    ag(way, s - 1, j, chip).wait_send()
                    fw(way, s, j, chip, core).wait_send()
                    rs(way, s, j).wait_send()

    for j in every:
        fw(0, 0, j, chip, core).wait_send()
        sib_copy(j).wait_send()
        fin_copy(j).wait_send()

    @pl.loop(1, far)
    def _(s):
        sent(s, False)

    sent(far, True)


def on_device(n, tokens, norm_gain, w_expand, b_expand, w_project, b_project):
    rows, width = tokens.shape
    units = w_expand.shape[1]
    chips = n // 2
    far = chips // 2
    pair, total = 2 * rows, rows * n
    half = width // 2
    wide = half // CHUNKS
    wire = BF16 if chips <= 8 else F32
    dma = pltpu.SemaphoreType.DMA
    vmem = pl.BlockSpec(memory_space=pltpu.VMEM)
    hbm = pl.BlockSpec(memory_space=pl.ANY)
    return pl.pallas_call(
        functools.partial(kernel, n),
        out_shape=jax.ShapeDtypeStruct((rows, width), BF16),
        in_specs=[vmem] * 4 + [hbm] * 2,
        out_specs=vmem,
        scratch_shapes=[
            pltpu.VMEM((width, units), BF16),
            pltpu.VMEM((units, width), BF16),
            pltpu.VMEM((n, CHUNKS, pair, wide), BF16),
            pltpu.VMEM((2, total, half), BF16),
            pltpu.VMEM((total, units), BF16),
            pltpu.VMEM((CHUNKS, total, wide), BF16),
            pltpu.VMEM((CHUNKS, total, wide), BF16),
            pltpu.VMEM((CHUNKS, total, wide), F32),
            pltpu.VMEM((2, far, CHUNKS, pair, wide), wire),
            pltpu.VMEM((2, far, CHUNKS, pair, wide), wire),
            pltpu.VMEM((CHUNKS, 2, rows, wide), F32),
            pltpu.VMEM((CHUNKS, rows, wide), F32),
            dma((2,)),
            dma((2,)),
            dma((2, far, CHUNKS)),
            dma((2, far, CHUNKS)),
            dma((2, far + 1, CHUNKS)),
            dma((2, far + 1, CHUNKS)),
            dma((CHUNKS,)),
            dma((CHUNKS,)),
            dma((2, far, CHUNKS)),
            dma((2, far, CHUNKS)),
            dma((CHUNKS,)),
            dma((CHUNKS,)),
        ],
        compiler_params=pltpu.CompilerParams(
            collective_id=0, has_side_effects=True, vmem_limit_bytes=60 * 1024 * 1024
        ),
    )(tokens, norm_gain[None], b_expand[None], b_project[None], w_expand, w_project)


def solution(mesh):
    placed = (P(("groups", "blk"), None), P(), P(None, "blk"), P("blk"), P("blk", None), P())
    return jax.shard_map(
        functools.partial(on_device, mesh.shape["blk"]),
        mesh=mesh, in_specs=placed, out_specs=P(("groups", "blk"), None), check_vma=False,
    )
```

time: 62.8 us -> 45 us (0.72)
  Pallas kernels: 59.8 us -> 42 us
    pallas_call x1, Pallas kernels: 59.8 us -> 42 us  [on_device(): pl.pallas_call(functools.partial(kernel, n), out_shape=jax.ShapeDtypeStru...]
where the time goes in v2:
time: 45 us; the launch traced here: 44.8 us
  Pallas kernels  42 us (93%)
  local copies, waits for them, and re-layouts  2.83 us (6%)
    pallas_call x1, Pallas kernels, on_device(): pl.pallas_call(functools.partial(kernel, n), out_shape=jax.ShapeDtypeStru...  42 us
    unnamed x1, local copies, waits for them, and re-layouts  1.54 us
    broadcast_in_dim x1, local copies, waits for them, and re-layouts, on_device(): b_expand[None]  1.29 us

profile of v2, /device:TPU:0, one launch (start us, length us, event | category | flops | bytes accessed | tf_op | source)
XLA Modules:
  0.0 44.8 jit_solution(7777480776105079363)
XLA Ops:
  0.0 1.3 %broadcast_in_dim.10.b1 = f32[1,1536]{1,0:T(1,128)} reshape(f32[1536]{0:T(1024)} %param.9) | data formatting | bytes 12288 | tf_op jit(solution)/shard_map/broadcast_in_dim | solution.py:323
  1.3 42.0 %shard_map.64 = bf16[8,6144]{1,0:T(8,128)(2,1)} custom-call(bf16[8,6144]{1,0:T(8,128)(2,1)} %tok.1, f32[1,6144]{1,0:T(1,128)} %bitcast.2, f32[1,1536]{1,0:T(1,128)} %broadcast_in_dim.10.b1, f32[1,6144]{1,0:T(1,128)} %bitcast.3, bf16[6144,1536]{1,0:T(8,128)(2,1)} %w1.1, bf16[1536,6144]{1,0:T(8,128)(2,1)} %w2.1), custom_call_target="tpu_custom_call" | custom-call | tf_op jit(solution)/shard_map/pallas_call | solution.py:289
  43.3 1.5 %copy.8 = bf16[8,6144]{1,0:T(8,128)(2,1)} copy(bf16[8,6144]{1,0:T(8,128)(2,1)} %shard_map.64) | data formatting | bytes 196608

commit v3 on v2

--- a/solution.py
+++ b/solution.py
@@ -37,8 +37,8 @@
 
 def kernel(
     n, tok, gain, b1, b2, w1, w2, out,
-    w1v, w2v, xin, lhs, hid, snd, sib_in, own, ring_in, ring_out, fin, fin_in,
-    w1_sem, w2_sem, ag_send, ag_recv, fw_send, fw_recv, sib_send, sib_recv, rs_send, rs_recv, fin_send, fin_recv,
+    w1v, w2v, xin, lhs, hid, snd, sib_in, own, ring_in, ring_out, last_in, last_out, ext_in,
+    w1_sem, w2_sem, ag_send, ag_recv, fw_send, fw_recv, sib_send, sib_recv, rs_send, rs_recv, last_send, last_recv, ext_send, ext_recv,
 ):
     rows, width = tok.shape
     pair = 2 * rows
@@ -59,6 +59,8 @@
 
     sign = (1, -1)
     ahead = [around(sign[w]) * 2 + core for w in ways]
+    beyond = [around(2 * sign[w]) * 2 + core for w in ways]
+    across = [around(sign[w]) * 2 + 1 - core for w in ways]
     sibling = chip * 2 + 1 - core
 
     def takes(way, j):
@@ -71,7 +73,7 @@
         )
 
     barrier = pltpu.get_barrier_semaphore()
-    for other in (*ahead, sibling):
+    for other in (*ahead, *across, *beyond, sibling):
         pl.semaphore_signal(barrier, inc=1, device_id={"blk": other}, device_id_type=pl.DeviceIdType.MESH)
 
     def w1_copy(h):
@@ -96,11 +98,11 @@
     for j in range(CHUNKS):
         xin[me, j] = folded[:, j * wide:(j + 1) * wide]
 
-    pl.semaphore_wait(barrier, 3)
-
-    def ag(way, s, j, where):
+    pl.semaphore_wait(barrier, 7)
+
+    def ag(way, s, j, where, leap=False):
         block = xin.at[where * 2 + core, j]
-        return send(block, block, ag_send.at[way, s, j], ag_recv.at[way, s, j], ahead[way])
+        return send(block, block, ag_send.at[way, s, j], ag_recv.at[way, s, j], (beyond if leap else ahead)[way])
 
     def fw(way, s, j, where, side):
         block = xin.at[where * 2 + side, j]
@@ -123,14 +125,16 @@
     for j in every:
         fw(0, 0, j, chip, core).start()
 
-    def gather(s, last, next_last):
+    def gather(s, onward, leap, last=False):
         for j in every:
             for way in ways:
                 if last and not takes(way, j):
                     continue
                 where = around(-sign[way] * s)
                 ag(way, s - 1, j, where).wait_recv()
-                if not last and (not next_last or takes(way, j)):
+                if leap and takes(way, j):
+                    ag(way, s + 1, j, where, True).start()
+                if onward:
                     ag(way, s, j, where).start()
                 fw(way, s, j, where, core).start()
 
@@ -142,20 +146,21 @@
                 fw(way, s, j, where, 1 - core).wait_recv()
             assemble(where, chunks)
 
-    gather(1, False, far == 2)
+    gather(1, True, False)
     for j in every:
         fw(0, 0, j, chip, 1 - core).wait_recv()
     assemble(chip, every)
 
-    @pl.loop(2, far - 1)
+    @pl.loop(2, far - 2)
     def _(s):
-        gather(s, False, False)
+        gather(s, True, False)
         take(s - 1, False)
 
-    if far > 2:
-        gather(far - 1, False, True)
-        take(far - 2, False)
-    gather(far, True, False)
+    gather(far - 2, True, True)
+    take(far - 3, False)
+    gather(far - 1, False, False)
+    gather(far, False, False, True)
+    take(far - 2, False)
     take(far - 1, False)
     take(far, True)
 
@@ -192,22 +197,54 @@
         project(1 - core, j, keep_theirs)
         sib_copy(j).start()
 
-    def rs(way, k, j):
+    def rs(way, k, j, leap=False):
         return send(
             ring_out.at[way, k - 1, j], ring_in.at[way, k - 1, j],
-            rs_send.at[way, k - 1, j], rs_recv.at[way, k - 1, j], ahead[way],
+            rs_send.at[way, k - 1, j], rs_recv.at[way, k - 1, j], (beyond if leap else ahead)[way],
         )
 
     def ours(j, where):
         return own[j, rows_of(where), :] + sib_in[j, rows_of(where), :].astype(F32)
 
-    def pass_on(way, k, j, more):
+    def came(way, k, j):
+        rs(way, k, j).wait_recv()
+        return ring_in[way, k - 1, j].astype(F32)
+
+    def running(way, k, j):
         total = ours(j, around(sign[way] * k))
-        if more:
-            rs(way, k + 1, j).wait_recv()
-            total += ring_in[way, k, j].astype(F32)
-        ring_out[way, k - 1, j] = total.astype(wire)
-        rs(way, k, j).start()
+        if isinstance(k, int) and k >= far - 1:
+            return total
+        total += came(way, k + 1, j)
+        if isinstance(k, int) and k == far - 2 and takes(way, j):
+            total += came(way, k + 2, j)
+        return total
+
+    def pass_on(way, k, j, leap=False):
+        ring_out[way, k - 1, j] = running(way, k, j).astype(wire)
+        rs(way, k, j, leap).start()
+
+    def last_copy(way, j, side):
+        to = around(sign[way]) * 2 + side
+        return send(
+            last_out.at[way, side, j], last_in.at[way, core, j],
+            last_send.at[way, side, j], last_recv.at[way, core, j], to,
+        )
+
+    def last_came(way, j, side):
+        return send(
+            last_out.at[way, 0, j], last_in.at[way, side, j],
+            last_send.at[way, 0, j], last_recv.at[way, side, j], sibling,
+        )
+
+    def fold(value):
+        return jnp.concatenate([value[:, :wide // 2], value[:, wide // 2:]], axis=0)
+
+    def unfold(value):
+        return jnp.concatenate([value[:rows], value[rows:]], axis=1)
+
+    def ext_copy(j):
+        theirs = pl.ds(pl.multiple_of(chip * pair + (1 - core) * rows, rows), rows)
+        return send(own.at[j, theirs], ext_in.at[j], ext_send.at[j], ext_recv.at[j], sibling)
 
     w2_copy(1).wait()
     for j in every:
@@ -219,40 +256,45 @@
         sib_copy(j).wait_recv()
         for way in ways:
             if takes(way, j):
-                pass_on(way, far, j, False)
-        for way in ways:
-            if not takes(way, j):
-                pass_on(way, far - 1, j, False)
-
-    for j in every:
-        for way in ways:
-            if takes(way, j):
-                pass_on(way, far - 1, j, True)
-
-    @pl.loop(2, far)
+                pass_on(way, far, j, True)
+        for way in ways:
+            pass_on(way, far - 1, j)
+        ext_copy(j).start()
+
+    if far > 3:
+        for j in every:
+            for way in ways:
+                pass_on(way, far - 2, j)
+
+    @pl.loop(3, far - 1)
     def _(s):
         for j in every:
             for way in ways:
-                pass_on(way, far - s, j, True)
-
-    def fin_copy(j):
-        return send(fin.at[j, 1 - core], fin_in.at[j], fin_send.at[j], fin_recv.at[j], sibling)
-
-    for j in every:
-        total = ours(j, chip)
-        for way in ways:
-            rs(way, 1, j).wait_recv()
-            total += ring_in[way, 0, j].astype(F32)
-        fin[j, 0] = total[:rows]
-        fin[j, 1] = total[rows:]
-        fin_copy(j).start()
-    for j in every:
-        fin_copy(j).wait_recv()
-    for g in range(2 * CHUNKS):
-        at = slice(g * wide, (g + 1) * wide)
-        j = g % CHUNKS
-        total = jnp.where(core == g // CHUNKS, fin[j, core], fin_in[j])
-        out[:, at] = (total + b2[:, at]).astype(BF16)
+                pass_on(way, far - s, j)
+
+    for j in every:
+        for way in ways:
+            total = running(way, 1, j)
+            for side in (0, 1):
+                last_out[way, side, j] = fold(total[side * rows:(side + 1) * rows]).astype(wire)
+                last_copy(way, j, side).start()
+
+    def my_rows(value):
+        return jnp.where(core == 0, value[:rows], value[rows:])
+
+    for j in every:
+        ext_copy(j).wait_recv()
+        mine = own[j, pl.ds(pl.multiple_of(chip * pair + core * rows, rows), rows), :]
+        mine += my_rows(sib_in[j, rows_of(chip), :].astype(F32))
+        other = my_rows(snd[j, rows_of(chip), :].astype(F32)) + ext_in[j]
+        for side in (0, 1):
+            start = side * half + j * wide
+            at = slice(start, start + wide)
+            total = jnp.where(core == side, mine, other) + b2[:, at]
+            for way in ways:
+                last_came(way, j, side).wait_recv()
+                total += unfold(last_in[way, side, j].astype(F32))
+            out[:, at] = total.astype(BF16)
 
     def sent(s, last):
         for j in every:
@@ -260,18 +302,31 @@
                 if not last or takes(way, j):
                     ag(way, s - 1, j, chip).wait_send()
                     fw(way, s, j, chip, core).wait_send()
-                    rs(way, s, j).wait_send()
+
+    def scattered(k, last):
+        for j in every:
+            for way in ways:
+                if not last or takes(way, j):
+                    rs(way, k, j).wait_send()
 
     for j in every:
         fw(0, 0, j, chip, core).wait_send()
         sib_copy(j).wait_send()
-        fin_copy(j).wait_send()
+        ext_copy(j).wait_send()
+        for way in ways:
+            for side in (0, 1):
+                last_copy(way, j, side).wait_send()
 
     @pl.loop(1, far)
     def _(s):
         sent(s, False)
 
+    @pl.loop(2, far)
+    def _(k):
+        scattered(k, False)
+
     sent(far, True)
+    scattered(far, True)
 
 
 def on_device(n, tokens, norm_gain, w_expand, b_expand, w_project, b_project):
@@ -302,7 +357,8 @@
             pltpu.VMEM((CHUNKS, total, wide), F32),
             pltpu.VMEM((2, far, CHUNKS, pair, wide), wire),
             pltpu.VMEM((2, far, CHUNKS, pair, wide), wire),
-            pltpu.VMEM((CHUNKS, 2, rows, wide), F32),
+            pltpu.VMEM((2, 2, CHUNKS, pair, wide // 2), wire),
+            pltpu.VMEM((2, 2, CHUNKS, pair, wide // 2), wire),
             pltpu.VMEM((CHUNKS, rows, wide), F32),
             dma((2,)),
             dma((2,)),
@@ -314,6 +370,8 @@
             dma((CHUNKS,)),
             dma((2, far, CHUNKS)),
             dma((2, far, CHUNKS)),
+            dma((2, 2, CHUNKS)),
+            dma((2, 2, CHUNKS)),
             dma((CHUNKS,)),
             dma((CHUNKS,)),
         ],

time: 45 us -> 42.4 us (0.942)
  Pallas kernels: 42 us -> 39.3 us
    pallas_call x1, Pallas kernels: 42 us -> 39.3 us  [on_device(): pl.pallas_call(functools.partial(kernel, n), out_shape=jax.ShapeDtypeStru...]
where the time goes in v3:
time: 42.4 us; the launch traced here: 42.2 us
  Pallas kernels  39.3 us (93%)
  local copies, waits for them, and re-layouts  2.83 us (7%)
    pallas_call x1, Pallas kernels, on_device(): pl.pallas_call(functools.partial(kernel, n), out_shape=jax.ShapeDtypeStru...  39.3 us
    unnamed x1, local copies, waits for them, and re-layouts  1.54 us
    broadcast_in_dim x1, local copies, waits for them, and re-layouts, on_device(): b_expand[None]  1.29 us

profile of v3, /device:TPU:0, one launch (start us, length us, event | category | flops | bytes accessed | tf_op | source)
XLA Modules:
  0.0 42.2 jit_solution(5899377357604997621)
XLA Ops:
  0.0 1.3 %broadcast_in_dim.10.b1 = f32[1,1536]{1,0:T(1,128)} reshape(f32[1536]{0:T(1024)} %param.9) | data formatting | bytes 12288 | tf_op jit(solution)/shard_map/broadcast_in_dim | solution.py:381
  1.3 39.3 %shard_map.64 = bf16[8,6144]{1,0:T(8,128)(2,1)} custom-call(bf16[8,6144]{1,0:T(8,128)(2,1)} %tok.1, f32[1,6144]{1,0:T(1,128)} %bitcast.2, f32[1,1536]{1,0:T(1,128)} %broadcast_in_dim.10.b1, f32[1,6144]{1,0:T(1,128)} %bitcast.3, bf16[6144,1536]{1,0:T(8,128)(2,1)} %w1.1, bf16[1536,6144]{1,0:T(8,128)(2,1)} %w2.1), custom_call_target="tpu_custom_call" | custom-call | tf_op jit(solution)/shard_map/pallas_call | solution.py:344
  40.6 1.5 %copy.8 = bf16[8,6144]{1,0:T(8,128)(2,1)} copy(bf16[8,6144]{1,0:T(8,128)(2,1)} %shard_map.64) | data formatting | bytes 196608

commit v4 on v3

--- a/solution.py
+++ b/solution.py
@@ -8,7 +8,7 @@
 from jax.sharding import PartitionSpec as P
 
 F32, BF16 = jnp.float32, jnp.bfloat16
-CHUNKS = 2
+CHUNKS = 4
 
 
 def gelu_tanh(value):
@@ -174,7 +174,8 @@
         at = pl.ds(pl.multiple_of(t * tile, tile), tile)
         total = jnp.dot(lhs[0], w1v[:half, at], preferred_element_type=F32)
         total += jnp.dot(lhs[1], w1v[half:, at], preferred_element_type=F32)
-        hid[:, at] = gelu_tanh(total + b1[:, at]).astype(BF16)
+        bias = [b1[pl.ds(t * (tile // 128) + i, 1), :] for i in range(tile // 128)]
+        hid[:, at] = gelu_tanh(total + jnp.concatenate(bias, axis=1)).astype(BF16)
 
     cut = tile_of(wide)
 
@@ -378,7 +379,7 @@
         compiler_params=pltpu.CompilerParams(
             collective_id=0, has_side_effects=True, vmem_limit_bytes=60 * 1024 * 1024
         ),
-    )(tokens, norm_gain[None], b_expand[None], b_project[None], w_expand, w_project)
+    )(tokens, norm_gain[None], b_expand.reshape(units // 128, 128), b_project[None], w_expand, w_project)
 
 
 def solution(mesh):

time: 42.4 us -> 40.1 us (0.946)
  local copies, waits for them, and re-layouts: 2.83 us -> 1.54 us
  Pallas kernels: 39.3 us -> 38.3 us
    broadcast_in_dim x1 -> x0, local copies, waits for them, and re-layouts: 1.29 us -> none  [on_device(): b_expand[None]]
    pallas_call x1, Pallas kernels: 39.3 us -> 38.3 us  [on_device(): pl.pallas_call(functools.partial(kernel, n), out_shape=jax.ShapeDtypeStru...]
where the time goes in v4:
time: 40.1 us; the launch traced here: 39.9 us
  Pallas kernels  38.3 us (96%)
  local copies, waits for them, and re-layouts  1.54 us (4%)
    pallas_call x1, Pallas kernels, on_device(): pl.pallas_call(functools.partial(kernel, n), out_shape=jax.ShapeDtypeStru...  38.3 us
    unnamed x1, local copies, waits for them, and re-layouts  1.54 us

profile of v4, /device:TPU:0, one launch (start us, length us, event | category | flops | bytes accessed | tf_op | source)
XLA Modules:
  0.0 39.9 jit_solution(15511186218408607419)
XLA Ops:
  0.0 38.3 %shard_map.64 = bf16[8,6144]{1,0:T(8,128)(2,1)} custom-call(bf16[8,6144]{1,0:T(8,128)(2,1)} %tok.1, f32[1,6144]{1,0:T(1,128)} %bitcast.3, f32[12,128]{1,0:T(8,128)} %bitcast.5, f32[1,6144]{1,0:T(1,128)} %bitcast.4, bf16[6144,1536]{1,0:T(8,128)(2,1)} %w1.1, bf16[1536,6144]{1,0:T(8,128)(2,1)} %w2.1), custom_call_target="tpu_custom_call" | custom-call | tf_op jit(solution)/shard_map/pallas_call | solution.py:345
  38.4 1.5 %copy.8 = bf16[8,6144]{1,0:T(8,128)(2,1)} copy(bf16[8,6144]{1,0:T(8,128)(2,1)} %shard_map.64) | data formatting | bytes 196608
